TPU v7x, 512 devices: a whole 4x8x8 slice. The times are simulated.
512 devices in a mesh: tm: 32 (over y, x), space: 16 (over z, core).
Axes of the slice: x: 4, y: 8, z: 8, core: 2. Of those that a mesh axis runs over, the one named last changes fastest.
Arguments:
- local_term: float32 [32, 512, 512], P('tm', 'space'), may hold values from -2 to 16, as said below
- coupling: float32 [32, 512, 512], P('tm', 'space'), may hold values from -0.25 to 1.2
Outputs:
- sigma: float32 [32, 512, 512], P('tm', 'space')
Inputs may be any that keep to these rules, and one draw needn't show every extreme that they name: local_term[t] is symmetric for every time block t.
All inputs are finite; a program needn't handle non-finite values.
Results may differ from a plain program's by a relative error of at most 0.00014.
Values sent between devices are 32-bit elements; how exact they have to be, the bound alone decides.
No kernel may reach another device: no remote copies, remote signals or barrier semaphores. Data moves between devices by JAX's collectives and lax.ppermute only.
A program may use at most 64 MiB of HBM per device.

v0:
```python
import jax
import jax.numpy as jnp
from jax import lax
from jax.sharding import PartitionSpec as P

HIGH = lax.Precision.HIGHEST


def from_behind(shard, axis, by):
    peers = lax.axis_size(axis)
    pairs = [(i, i + by) for i in range(peers) if 0 <= i + by < peers]
    return lax.ppermute(shard, axis, pairs)


def matmul(left, right):
    return jnp.dot(left, right, precision=HIGH, preferred_element_type=jnp.float32)


def inner_rows(left, right):
    return lax.dot_general(
        left, right, (((0,), (0,)), ((), ())), precision=HIGH, preferred_element_type=jnp.float32
    )


def combine(terms, maps, later_terms, later_maps, owner):
    rows, width = terms.shape

    def accumulate(piece):
        product = matmul(later_terms, piece)
        if later_maps is None:
            return (product,)
        return (product, matmul(later_maps, piece))

    folded = accumulate(lax.all_gather(maps, "space", axis=0, tiled=True))
    weighted = folded[0]
    own_columns = lax.dynamic_slice_in_dim(
        lax.all_gather(maps, "space", axis=0, tiled=True), owner * rows, rows, 1
    )
    congruence = inner_rows(own_columns, lax.all_gather(weighted, "space", axis=0, tiled=True))
    new_terms = terms + congruence
    new_maps = None if later_maps is None else folded[1]
    return (new_terms, new_maps)


def local(local_term, coupling):
    terms = local_term[0]
    maps = coupling[0]
    count_tm = lax.axis_size("tm")
    levels = (count_tm - 1).bit_length()
    owner = lax.axis_index("space")
    for level in range(levels):
        offset = 1 << level
        if level == levels - 1:
            later_terms = from_behind(terms, "tm", -offset)
            later_maps = None
        else:
            later_terms, later_maps = from_behind((terms, maps), "tm", -offset)
        terms, maps = combine(terms, maps, later_terms, later_maps, owner)
    return terms[None]


def solution(mesh):
    placed = (P("tm", "space", None), P("tm", "space", None))
    return jax.shard_map(
        local, mesh=mesh, in_specs=placed, out_specs=P("tm", "space", None), check_vma=False
    )
```

profile of v0, /device:TPU:1, one launch (start us, length us, event | category | flops | bytes accessed | tf_op | source)
XLA Modules:
  0.0 450.1 jit_solution(3637459121479575733)
XLA Ops:
  6.5 0.7 all-gather.30.cloned.1.call-update
  7.3 0.1 copy-done.8
  7.4 1.3 collective-permute-start
  8.7 4.3 collective-permute-done
  13.0 44.4 %all-gather.30.cloned.1.call-done = f32[1,512,512]{2,1,0:T(8,128)} async-done(((f32[1,32,512]{2,1,0:T(8,128)}), f32[1,512,512]{2,1,0:T(8,128)}) %all-gather.30.cloned.1.call-update) | async-done | bytes 1048592 | tf_op jit(solution)/shard_map/all_gather | solution.py:37
  57.4 2.6 fusion.1
  60.1 0.8 copy-done.7
  60.9 1.3 collective-permute-start.1
  62.1 3.7 collective-permute-done.1
  65.9 1.3 fusion.3
  67.3 33.0 %all-gather.12.cloned.1.call-done = f32[512,512]{1,0:T(8,128)} async-done(((f32[32,512]{1,0:T(8,128)}), f32[512,512]{1,0:T(8,128)}) %all-gather.12.cloned.1.call-update) | async-done | bytes 1048592 | tf_op jit(solution)/shard_map/all_gather | solution.py:39
  100.3 2.0 convolution_add_fusion.4
  102.2 1.3 collective-permute-start.2
  103.5 39.0 %all-gather.14.cloned.1.call-done = f32[512,512]{1,0:T(8,128)} async-done(((f32[32,512]{1,0:T(8,128)}), f32[512,512]{1,0:T(8,128)}) %all-gather.14.cloned.1.call-update) | async-done | bytes 1048592 | tf_op jit(solution)/shard_map/all_gather | solution.py:37
  142.5 2.6 fusion.16
  145.2 0.0 all-gather.18.cloned.1.call-start
  145.2 0.8 copy-done.4
  146.0 1.3 collective-permute-start.3
  147.3 5.2 %collective-permute-done.3 = f32[32,512]{1,0:T(8,128)S(1)} collective-permute-done((f32[32,512]{1,0:T(8,128)S(1)}, f32[32,512]{1,0:T(8,128)S(1)}, u32[]{:S(2)}, u32[]{:S(2)}) %collective-permute-start.3) | collective-permute-done | bytes 65568 | tf_op jit(solution)/shard_map/ppermute | solution.py:12
  152.5 1.3 fusion.17
  153.9 31.5 %all-gather.16.cloned.1.call-done = f32[512,512]{1,0:T(8,128)} async-done(((f32[32,512]{1,0:T(8,128)}), f32[512,512]{1,0:T(8,128)}) %all-gather.16.cloned.1.call-update) | async-done | bytes 1048592 | tf_op jit(solution)/shard_map/all_gather | solution.py:39
  185.4 2.0 convolution_add_fusion.3
  187.4 1.3 collective-permute-start.4
  188.7 38.8 %all-gather.18.cloned.1.call-done = f32[512,512]{1,0:T(8,128)} async-done(((f32[32,512]{1,0:T(8,128)}), f32[512,512]{1,0:T(8,128)}) %all-gather.18.cloned.1.call-update) | async-done | bytes 1048592 | tf_op jit(solution)/shard_map/all_gather | solution.py:37
  227.5 2.6 fusion.18
  230.2 0.0 all-gather.22.cloned.1.call-start
  230.2 0.8 copy-done.5
  231.0 1.3 collective-permute-start.5
  232.3 3.7 collective-permute-done.5
  236.0 1.3 fusion.19
  237.3 0.0 all-gather.24.cloned.1.call-start
  237.4 33.0 %all-gather.20.cloned.1.call-done = f32[512,512]{1,0:T(8,128)} async-done(((f32[32,512]{1,0:T(8,128)}), f32[512,512]{1,0:T(8,128)}) %all-gather.20.cloned.1.call-update) | async-done | bytes 1048592 | tf_op jit(solution)/shard_map/all_gather | solution.py:39
  270.4 2.0 convolution_add_fusion.2
  272.4 1.3 collective-permute-start.6
  273.7 39.0 %all-gather.22.cloned.1.call-done = f32[512,512]{1,0:T(8,128)} async-done(((f32[32,512]{1,0:T(8,128)}), f32[512,512]{1,0:T(8,128)}) %all-gather.22.cloned.1.call-update) | async-done | bytes 1048592 | tf_op jit(solution)/shard_map/all_gather | solution.py:37
  312.6 2.6 fusion.20
  315.3 0.0 all-gather.26.cloned.1.call-start
  315.3 0.8 copy-done.6
  316.1 1.3 collective-permute-start.7
  317.4 4.6 %collective-permute-done.7 = f32[32,512]{1,0:T(8,128)S(1)} collective-permute-done((f32[32,512]{1,0:T(8,128)S(1)}, f32[32,512]{1,0:T(8,128)S(1)}, u32[]{:S(2)}, u32[]{:S(2)}) %collective-permute-start.7) | collective-permute-done | bytes 65568 | tf_op jit(solution)/shard_map/ppermute | solution.py:12
  322.0 1.3 fusion.21
  323.4 32.1 %all-gather.24.cloned.1.call-done = f32[512,512]{1,0:T(8,128)} async-done(((f32[32,512]{1,0:T(8,128)}), f32[512,512]{1,0:T(8,128)}) %all-gather.24.cloned.1.call-update) | async-done | bytes 1048592 | tf_op jit(solution)/shard_map/all_gather | solution.py:39
  355.5 2.0 convolution_add_fusion.1
  357.5 1.3 collective-permute-start.8
  358.8 39.0 %all-gather.26.cloned.1.call-done = f32[512,512]{1,0:T(8,128)} async-done(((f32[32,512]{1,0:T(8,128)}), f32[512,512]{1,0:T(8,128)}) %all-gather.26.cloned.1.call-update) | async-done | bytes 1048592 | tf_op jit(solution)/shard_map/all_gather | solution.py:37
  397.8 2.6 fusion.22
  400.3 40.2 %all-gather.28.cloned.1.call-done = f32[512,512]{1,0:T(8,128)} async-done(((f32[32,512]{1,0:T(8,128)}), f32[512,512]{1,0:T(8,128)}) %all-gather.28.cloned.1.call-update) | async-done | bytes 1048592 | tf_op jit(solution)/shard_map/all_gather | solution.py:39
  440.6 2.7 fusion
  (32 shorter events, 0.4 us)
Async XLA Ops:
  6.5 0.8 copy-start.8
  6.5 50.8 %all-gather.30.cloned.1.call-start = ((), (), s32[]{:S(2)}) async-start(), calls=%async_computation.9 | async-start | bytes 1114112 | tf_op jit(solution)/shard_map/all_gather | solution.py:37
  7.3 93.0 %all-gather.12.cloned.1.call-start = ((), (), s32[]{:S(2)}) async-start(), calls=%async_computation | async-start | bytes 1114112 | tf_op jit(solution)/shard_map/all_gather | solution.py:39
  7.4 5.6 %collective-permute-start = (f32[32,512]{1,0:T(8,128)S(1)}, f32[32,512]{1,0:T(8,128)S(1)}, u32[]{:S(2)}, u32[]{:S(2)}) collective-permute-start(f32[32,512]{1,0:T(8,128)S(1)} %bitcast.35), channel_id=1, source_target_pairs={{16,0},{32,16},{48,32},{64,48},{80,64},{96,80},{112,96},{128,112},... | collective-permute-start | bytes 196616 | tf_op jit(solution)/shard_map/ppermute | solution.py:12
  57.4 8.5 %copy-start.1 = (f32[1,512,512]{2,1,0:T(8,128)S(1)}, f32[1,512,512]{2,1,0:T(8,128)}, u32[]{:S(2)}) copy-start(f32[1,512,512]{2,1,0:T(8,128)} %all-gather.30.cloned.1.call-done) | copy-start | bytes 3145732
  60.0 0.8 copy-start.7
  60.0 82.5 %all-gather.14.cloned.1.call-start = ((), (), s32[]{:S(2)}) async-start(), calls=%async_computation.1 | async-start | bytes 1114112 | tf_op jit(solution)/shard_map/all_gather | solution.py:37
  60.9 5.0 %collective-permute-start.1 = (f32[32,512]{1,0:T(8,128)S(1)}, f32[32,512]{1,0:T(8,128)S(1)}, u32[]{:S(2)}, u32[]{:S(2)}) collective-permute-start(f32[32,512]{1,0:T(8,128)S(1)} %bitcast.34), channel_id=1, source_target_pairs={{16,0},{32,16},{48,32},{64,48},{80,64},{96,80},{112,96},{128,112},... | collective-permute-start | bytes 196616 | tf_op jit(solution)/shard_map/ppermute | solution.py:12
  67.2 118.2 %all-gather.16.cloned.1.call-start = ((), (), s32[]{:S(2)}) async-start(), calls=%async_computation.2 | async-start | bytes 1114112 | tf_op jit(solution)/shard_map/all_gather | solution.py:39
  102.2 40.3 %collective-permute-start.2 = (f32[32,512]{1,0:T(8,128)S(1)}, f32[32,512]{1,0:T(8,128)S(1)}, u32[]{:S(2)}, u32[]{:S(2)}) collective-permute-start(f32[32,512]{1,0:T(8,128)S(1)} %convolution_add_fusion.4), channel_id=1, source_target_pairs={{32,0},{48,16},{64,32},{80,48},{96,64},{112,80},{128,96},{144,112}... | collective-permute-start | bytes 196616 | tf_op jit(solution)/shard_map/ppermute | solution.py:12
  142.5 10.0 %copy-start = (f32[512,512]{1,0:T(8,128)S(1)}, f32[512,512]{1,0:T(8,128)}, u32[]{:S(2)}) copy-start(f32[512,512]{1,0:T(8,128)} %all-gather.14.cloned.1.call-done) | copy-start | bytes 3145732
  145.2 0.8 copy-start.4
  145.2 82.3 %all-gather.18.cloned.1.call-start = ((), (), s32[]{:S(2)}) async-start(), calls=%async_computation.3 | async-start | bytes 1114112 | tf_op jit(solution)/shard_map/all_gather | solution.py:37
  146.0 6.5 %collective-permute-start.3 = (f32[32,512]{1,0:T(8,128)S(1)}, f32[32,512]{1,0:T(8,128)S(1)}, u32[]{:S(2)}, u32[]{:S(2)}) collective-permute-start(f32[32,512]{1,0:T(8,128)S(1)} %copy-done.4), channel_id=1, source_target_pairs={{32,0},{48,16},{64,32},{80,48},{96,64},{112,80},{128,96},{144,112}... | collective-permute-start | bytes 196616 | tf_op jit(solution)/shard_map/ppermute | solution.py:12
  153.8 116.6 %all-gather.20.cloned.1.call-start = ((), (), s32[]{:S(2)}) async-start(), calls=%async_computation.4 | async-start | bytes 1114112 | tf_op jit(solution)/shard_map/all_gather | solution.py:39
  187.4 40.1 %collective-permute-start.4 = (f32[32,512]{1,0:T(8,128)S(1)}, f32[32,512]{1,0:T(8,128)S(1)}, u32[]{:S(2)}, u32[]{:S(2)}) collective-permute-start(f32[32,512]{1,0:T(8,128)S(1)} %convolution_add_fusion.3), channel_id=1, source_target_pairs={{64,0},{80,16},{96,32},{112,48},{128,64},{144,80},{160,96},{176,11... | collective-permute-start | bytes 196616 | tf_op jit(solution)/shard_map/ppermute | solution.py:12
  227.5 8.5 %copy-start.2 = (f32[512,512]{1,0:T(8,128)S(1)}, f32[512,512]{1,0:T(8,128)}, u32[]{:S(2)}) copy-start(f32[512,512]{1,0:T(8,128)} %all-gather.18.cloned.1.call-done) | copy-start | bytes 3145732
  230.1 0.8 copy-start.5
  230.2 82.5 %all-gather.22.cloned.1.call-start = ((), (), s32[]{:S(2)}) async-start(), calls=%async_computation.5 | async-start | bytes 1114112 | tf_op jit(solution)/shard_map/all_gather | solution.py:37
  231.0 5.0 %collective-permute-start.5 = (f32[32,512]{1,0:T(8,128)S(1)}, f32[32,512]{1,0:T(8,128)S(1)}, u32[]{:S(2)}, u32[]{:S(2)}) collective-permute-start(f32[32,512]{1,0:T(8,128)S(1)} %copy-done.5), channel_id=1, source_target_pairs={{64,0},{80,16},{96,32},{112,48},{128,64},{144,80},{160,96},{176,11... | collective-permute-start | bytes 196616 | tf_op jit(solution)/shard_map/ppermute | solution.py:12
  237.3 118.2 %all-gather.24.cloned.1.call-start = ((), (), s32[]{:S(2)}) async-start(), calls=%async_computation.6 | async-start | bytes 1114112 | tf_op jit(solution)/shard_map/all_gather | solution.py:39
  272.4 40.3 %collective-permute-start.6 = (f32[32,512]{1,0:T(8,128)S(1)}, f32[32,512]{1,0:T(8,128)S(1)}, u32[]{:S(2)}, u32[]{:S(2)}) collective-permute-start(f32[32,512]{1,0:T(8,128)S(1)} %convolution_add_fusion.2), channel_id=1, source_target_pairs={{128,0},{144,16},{160,32},{176,48},{192,64},{208,80},{224,96},{240... | collective-permute-start | bytes 196616 | tf_op jit(solution)/shard_map/ppermute | solution.py:12
  312.6 9.4 %copy-start.3 = (f32[512,512]{1,0:T(8,128)S(1)}, f32[512,512]{1,0:T(8,128)}, u32[]{:S(2)}) copy-start(f32[512,512]{1,0:T(8,128)} %all-gather.22.cloned.1.call-done) | copy-start | bytes 3145732
  315.3 0.8 copy-start.6
  315.3 82.5 %all-gather.26.cloned.1.call-start = ((), (), s32[]{:S(2)}) async-start(), calls=%async_computation.7 | async-start | bytes 1114112 | tf_op jit(solution)/shard_map/all_gather | solution.py:37
  316.1 5.9 %collective-permute-start.7 = (f32[32,512]{1,0:T(8,128)S(1)}, f32[32,512]{1,0:T(8,128)S(1)}, u32[]{:S(2)}, u32[]{:S(2)}) collective-permute-start(f32[32,512]{1,0:T(8,128)S(1)} %copy-done.6), channel_id=1, source_target_pairs={{128,0},{144,16},{160,32},{176,48},{192,64},{208,80},{224,96},{240... | collective-permute-start | bytes 196616 | tf_op jit(solution)/shard_map/ppermute | solution.py:12
  323.4 117.2 %all-gather.28.cloned.1.call-start = ((), (), s32[]{:S(2)}) async-start(), calls=%async_computation.8 | async-start | bytes 1114112 | tf_op jit(solution)/shard_map/all_gather | solution.py:39
  357.5 40.3 %collective-permute-start.8 = (f32[32,512]{1,0:T(8,128)S(1)}, f32[32,512]{1,0:T(8,128)S(1)}, u32[]{:S(2)}, u32[]{:S(2)}) collective-permute-start(f32[32,512]{1,0:T(8,128)S(1)} %convolution_add_fusion.1), channel_id=1, source_target_pairs={{256,0},{272,16},{288,32},{304,48},{320,64},{336,80},{352,96},{368... | collective-permute-start | bytes 196616 | tf_op jit(solution)/shard_map/ppermute | solution.py:12
Sparse Core Ops, SparseCore 0:
  9.5 47.8 all-gather.29
  60.2 40.0 all-gather.11
  102.4 40.0 all-gather.13
  145.3 40.0 all-gather.15
  187.4 40.0 all-gather.17
  230.3 40.0 all-gather.19
  272.5 40.0 all-gather.21
  315.4 40.0 all-gather.23
  357.7 40.0 all-gather.25
  400.5 40.0 all-gather.27
where the time goes:
time: 451 us; the launch traced here: 450 us
  waiting for transfers between devices  392 us (87%)
  matrix products  28.9 us (6%)
  between operations  13.7 us (3%)
  starting transfers between devices  11.9 us (3%)
    all_gather x5, waiting for transfers between devices, combine(): lax.all_gather(maps, 'space', axis=0, tiled=True)  200 us
    all_gather x5, waiting for transfers between devices, combine(): lax.all_gather(weighted, 'space', axis=0, tiled=True)  170 us
    ppermute x9, waiting for transfers between devices, from_behind(): return lax.ppermute(shard, axis, pairs)  21.6 us
    dot_general x9, matrix products, matmul(): jnp.dot(left, right, precision=HIGH, preferred_element_type=jnp.float32)  18.4 us
    ppermute x9, starting transfers between devices, from_behind(): return lax.ppermute(shard, axis, pairs)  11.6 us
    dot_general x5, matrix products, inner_rows(): lax.dot_general(left, right, (((0,), (0,)), ((), ())), precision=HIGH, pr...  10.5 us
  transfers between devices with their start and end apart: 19, of which 15 were waited for; matrix products, arithmetic and copies ran while one was open for 3% of the time, Pallas kernels for 0%

commit v1 on v0

--- a/solution.py
+++ b/solution.py
@@ -34,7 +34,12 @@
     folded = accumulate(lax.all_gather(maps, "space", axis=0, tiled=True))
     weighted = folded[0]
     own_columns = lax.dynamic_slice_in_dim(
-        lax.all_gather(maps, "space", axis=0, tiled=True), owner * rows, rows, 1
+        jnp.concatenate(
+            lax.all_to_all(jnp.stack([maps] * lax.axis_size("space")), "space", 0, 0), axis=0
+        ),
+        owner * rows,
+        rows,
+        1,
     )
     congruence = inner_rows(own_columns, lax.all_gather(weighted, "space", axis=0, tiled=True))
     new_terms = terms + congruence

time: 451 us -> 487 us (1.080)
  starting transfers between devices: 11.9 us -> 34.9 us
  waiting for transfers between devices: 392 us -> 399 us
  local copies, waits for them, and re-layouts: 3.15 us -> 8.93 us
    all_to_all x0 -> x5, waiting for transfers between devices: none -> 92.4 us  [combine(): lax.all_to_all(jnp.stack([maps] * lax.axis_size('space')), 'space', 0, 0)]
    all_gather x5, waiting for transfers between devices: 170 us -> 81.7 us  [combine(): lax.all_gather(weighted, 'space', axis=0, tiled=True)]
    all_to_all x0 -> x5, starting transfers between devices: none -> 23 us  [combine(): lax.all_to_all(jnp.stack([maps] * lax.axis_size('space')), 'space', 0, 0)]
    another operation x0 -> x5, local copies, waits for them, and re-layouts: none -> 5.58 us  [combine(): jnp.stack([maps] * lax.axis_size('space'))]
  transfers between devices with their start and end apart: 19 -> 24, of which waited for: 15 -> 19; matrix products, arithmetic and copies ran while one was open for 3% -> 4% of each run, Pallas kernels for 0% -> 0%
where the time goes in v1:
time: 487 us; the launch traced here: 486 us
  waiting for transfers between devices  399 us (82%)
  starting transfers between devices  34.9 us (7%)
  matrix products  28.6 us (6%)
  between operations  13.7 us (3%)
  local copies, waits for them, and re-layouts  8.93 us (2%)
    all_gather x5, waiting for transfers between devices, combine(): folded = accumulate(lax.all_gather(maps, 'space', axis=0, tiled=True))  201 us
    all_to_all x5, waiting for transfers between devices, combine(): lax.all_to_all(jnp.stack([maps] * lax.axis_size('space')), 'space', 0, 0)  92.4 us
    all_gather x5, waiting for transfers between devices, combine(): lax.all_gather(weighted, 'space', axis=0, tiled=True)  81.7 us
    ppermute x9, waiting for transfers between devices, from_behind(): return lax.ppermute(shard, axis, pairs)  23.7 us
    all_to_all x5, starting transfers between devices, combine(): lax.all_to_all(jnp.stack([maps] * lax.axis_size('space')), 'space', 0, 0)  23 us
    dot_general x9, matrix products, matmul(): jnp.dot(left, right, precision=HIGH, preferred_element_type=jnp.float32)  18.1 us
    ppermute x9, starting transfers between devices, from_behind(): return lax.ppermute(shard, axis, pairs)  11.6 us
    dot_general x5, matrix products, inner_rows(): lax.dot_general(left, right, (((0,), (0,)), ((), ())), precision=HIGH, pr...  10.4 us
  transfers between devices with their start and end apart: 24, of which 19 were waited for; matrix products, arithmetic and copies ran while one was open for 4% of the time, Pallas kernels for 0%

profile of v1, /device:TPU:1, one launch (start us, length us, event | category | flops | bytes accessed | tf_op | source)
XLA Modules:
  0.0 485.6 jit_solution(15103898753872579437)
XLA Ops:
  7.4 1.3 collective-permute-start
  8.7 4.3 collective-permute-done
  13.0 44.4 %all-gather.30.cloned.1.call-done = f32[1,512,512]{2,1,0:T(8,128)} async-done(((f32[1,32,512]{2,1,0:T(8,128)}), f32[1,512,512]{2,1,0:T(8,128)}) %all-gather.30.cloned.1.call-update) | async-done | bytes 1048592 | tf_op jit(solution)/shard_map/all_gather | solution.py:34
  57.4 2.6 fusion.3
  61.9 4.6 all-to-all-start
  66.5 1.3 collective-permute-start.1
  67.8 4.3 collective-permute-done.1
  72.1 1.3 fusion.1
  73.5 23.7 %all-to-all-done = f32[16,32,512]{2,1,0:T(8,128)S(1)} async-done(((f32[16,32,512]{2,1,0:T(8,128)}), f32[16,32,512]{2,1,0:T(8,128)S(1)}, u32[]{:S(2)}, u32[]{:S(2)}) %all-to-all-start) | async-done | bytes 1048608 | tf_op jit(solution)/shard_map/all_to_all | solution.py:38
  97.2 9.5 %all-gather.12.cloned.1.call-done = f32[512,512]{1,0:T(8,128)} async-done(((f32[32,512]{1,0:T(8,128)}), f32[512,512]{1,0:T(8,128)}) %all-gather.12.cloned.1.call-update) | async-done | bytes 1048592 | tf_op jit(solution)/shard_map/all_gather | solution.py:44
  106.7 2.0 convolution_add_fusion.4
  108.7 1.3 collective-permute-start.2
  110.0 39.3 %all-gather.14.cloned.1.call-done = f32[512,512]{1,0:T(8,128)} async-done(((f32[32,512]{1,0:T(8,128)}), f32[512,512]{1,0:T(8,128)}) %all-gather.14.cloned.1.call-update) | async-done | bytes 1048592 | tf_op jit(solution)/shard_map/all_gather | solution.py:34
  149.3 2.6 fusion.15
  153.8 4.6 all-to-all-start.1
  158.4 1.3 collective-permute-start.3
  159.7 5.8 %collective-permute-done.3 = f32[32,512]{1,0:T(8,128)S(1)} collective-permute-done((f32[32,512]{1,0:T(8,128)S(1)}, f32[32,512]{1,0:T(8,128)S(1)}, u32[]{:S(2)}, u32[]{:S(2)}) %collective-permute-start.3) | collective-permute-done | bytes 65568 | tf_op jit(solution)/shard_map/ppermute | solution.py:12
  165.5 1.3 fusion.16
  166.9 22.2 %all-to-all-done.1 = f32[16,32,512]{2,1,0:T(8,128)S(1)} async-done(((f32[16,32,512]{2,1,0:T(8,128)}), f32[16,32,512]{2,1,0:T(8,128)S(1)}, u32[]{:S(2)}, u32[]{:S(2)}) %all-to-all-start.1) | async-done | bytes 1048608 | tf_op jit(solution)/shard_map/all_to_all | solution.py:38
  189.1 9.5 %all-gather.16.cloned.1.call-done = f32[512,512]{1,0:T(8,128)} async-done(((f32[32,512]{1,0:T(8,128)}), f32[512,512]{1,0:T(8,128)}) %all-gather.16.cloned.1.call-update) | async-done | bytes 1048592 | tf_op jit(solution)/shard_map/all_gather | solution.py:44
  198.6 2.0 convolution_add_fusion.3
  200.6 1.3 collective-permute-start.4
  201.9 39.2 %all-gather.18.cloned.1.call-done = f32[512,512]{1,0:T(8,128)} async-done(((f32[32,512]{1,0:T(8,128)}), f32[512,512]{1,0:T(8,128)}) %all-gather.18.cloned.1.call-update) | async-done | bytes 1048592 | tf_op jit(solution)/shard_map/all_gather | solution.py:34
  241.0 2.6 fusion.17
  245.5 4.6 all-to-all-start.2
  250.2 1.3 collective-permute-start.5
  251.5 4.3 collective-permute-done.5
  255.7 1.3 fusion.18
  257.1 23.7 %all-to-all-done.2 = f32[16,32,512]{2,1,0:T(8,128)S(1)} async-done(((f32[16,32,512]{2,1,0:T(8,128)}), f32[16,32,512]{2,1,0:T(8,128)S(1)}, u32[]{:S(2)}, u32[]{:S(2)}) %all-to-all-start.2) | async-done | bytes 1048608 | tf_op jit(solution)/shard_map/all_to_all | solution.py:38
  280.8 9.5 %all-gather.20.cloned.1.call-done = f32[512,512]{1,0:T(8,128)} async-done(((f32[32,512]{1,0:T(8,128)}), f32[512,512]{1,0:T(8,128)}) %all-gather.20.cloned.1.call-update) | async-done | bytes 1048592 | tf_op jit(solution)/shard_map/all_gather | solution.py:44
  290.3 2.0 convolution_add_fusion.2
  292.3 1.3 collective-permute-start.6
  293.6 39.3 %all-gather.22.cloned.1.call-done = f32[512,512]{1,0:T(8,128)} async-done(((f32[32,512]{1,0:T(8,128)}), f32[512,512]{1,0:T(8,128)}) %all-gather.22.cloned.1.call-update) | async-done | bytes 1048592 | tf_op jit(solution)/shard_map/all_gather | solution.py:34
  332.9 2.6 fusion.19
  337.4 4.6 all-to-all-start.3
  342.1 1.3 collective-permute-start.7
  343.4 5.2 %collective-permute-done.7 = f32[32,512]{1,0:T(8,128)S(1)} collective-permute-done((f32[32,512]{1,0:T(8,128)S(1)}, f32[32,512]{1,0:T(8,128)S(1)}, u32[]{:S(2)}, u32[]{:S(2)}) %collective-permute-start.7) | collective-permute-done | bytes 65568 | tf_op jit(solution)/shard_map/ppermute | solution.py:12
  348.5 1.3 fusion.20
  349.9 22.8 %all-to-all-done.3 = f32[16,32,512]{2,1,0:T(8,128)S(1)} async-done(((f32[16,32,512]{2,1,0:T(8,128)}), f32[16,32,512]{2,1,0:T(8,128)S(1)}, u32[]{:S(2)}, u32[]{:S(2)}) %all-to-all-start.3) | async-done | bytes 1048608 | tf_op jit(solution)/shard_map/all_to_all | solution.py:38
  372.7 9.5 %all-gather.24.cloned.1.call-done = f32[512,512]{1,0:T(8,128)} async-done(((f32[32,512]{1,0:T(8,128)}), f32[512,512]{1,0:T(8,128)}) %all-gather.24.cloned.1.call-update) | async-done | bytes 1048592 | tf_op jit(solution)/shard_map/all_gather | solution.py:44
  382.2 2.0 convolution_add_fusion.1
  384.2 1.3 collective-permute-start.8
  385.5 1.2 stack.14
  386.7 4.6 all-to-all-start.4
  391.3 38.5 %all-gather.26.cloned.1.call-done = f32[512,512]{1,0:T(8,128)} async-done(((f32[32,512]{1,0:T(8,128)}), f32[512,512]{1,0:T(8,128)}) %all-gather.26.cloned.1.call-update) | async-done | bytes 1048592 | tf_op jit(solution)/shard_map/all_gather | solution.py:34
  429.9 2.6 fusion.21
  432.5 43.7 %all-gather.28.cloned.1.call-done = f32[512,512]{1,0:T(8,128)} async-done(((f32[32,512]{1,0:T(8,128)}), f32[512,512]{1,0:T(8,128)}) %all-gather.28.cloned.1.call-update) | async-done | bytes 1048592 | tf_op jit(solution)/shard_map/all_gather | solution.py:44
  476.1 2.6 fusion
  (49 shorter events, 9.0 us)
Async XLA Ops:
  6.5 0.8 copy-start.9
  6.5 50.8 %all-gather.30.cloned.1.call-start = ((), (), s32[]{:S(2)}) async-start(), calls=%async_computation.14 | async-start | bytes 1114112 | tf_op jit(solution)/shard_map/all_gather | solution.py:34
  7.3 99.4 %all-gather.12.cloned.1.call-start = ((), (), s32[]{:S(2)}) async-start(), calls=%async_computation.5 | async-start | bytes 1114112 | tf_op jit(solution)/shard_map/all_gather | solution.py:44
  7.4 5.6 %collective-permute-start = (f32[32,512]{1,0:T(8,128)S(1)}, f32[32,512]{1,0:T(8,128)S(1)}, u32[]{:S(2)}, u32[]{:S(2)}) collective-permute-start(f32[32,512]{1,0:T(8,128)S(1)} %bitcast.43), channel_id=1, source_target_pairs={{16,0},{32,16},{48,32},{64,48},{80,64},{96,80},{112,96},{128,112},... | collective-permute-start | bytes 196616 | tf_op jit(solution)/shard_map/ppermute | solution.py:12
  59.9 0.8 copy-start.8
  61.9 10.2 %copy-start.3 = (f32[1,512,512]{2,1,0:T(8,128)S(1)}, f32[1,512,512]{2,1,0:T(8,128)}, u32[]{:S(2)}) copy-start(f32[1,512,512]{2,1,0:T(8,128)} %all-gather.30.cloned.1.call-done) | copy-start | bytes 3145732
  61.9 35.3 %all-to-all-start = ((f32[16,32,512]{2,1,0:T(8,128)}), f32[16,32,512]{2,1,0:T(8,128)S(1)}, u32[]{:S(2)}, u32[]{:S(2)}) async-start(f32[16,32,512]{2,1,0:T(8,128)} %stack.10), calls=%async_computation | async-start | bytes 2097152 | tf_op jit(solution)/shard_map/all_to_all | solution.py:38
  66.5 82.8 %all-gather.14.cloned.1.call-start = ((), (), s32[]{:S(2)}) async-start(), calls=%async_computation.6 | async-start | bytes 1114112 | tf_op jit(solution)/shard_map/all_gather | solution.py:34
  66.5 5.6 %collective-permute-start.1 = (f32[32,512]{1,0:T(8,128)S(1)}, f32[32,512]{1,0:T(8,128)S(1)}, u32[]{:S(2)}, u32[]{:S(2)}) collective-permute-start(f32[32,512]{1,0:T(8,128)S(1)} %bitcast.42), channel_id=1, source_target_pairs={{16,0},{32,16},{48,32},{64,48},{80,64},{96,80},{112,96},{128,112},... | collective-permute-start | bytes 196616 | tf_op jit(solution)/shard_map/ppermute | solution.py:12
  73.4 125.2 %all-gather.16.cloned.1.call-start = ((), (), s32[]{:S(2)}) async-start(), calls=%async_computation.7 | async-start | bytes 1114112 | tf_op jit(solution)/shard_map/all_gather | solution.py:44
  108.7 40.6 %collective-permute-start.2 = (f32[32,512]{1,0:T(8,128)S(1)}, f32[32,512]{1,0:T(8,128)S(1)}, u32[]{:S(2)}, u32[]{:S(2)}) collective-permute-start(f32[32,512]{1,0:T(8,128)S(1)} %convolution_add_fusion.4), channel_id=1, source_target_pairs={{32,0},{48,16},{64,32},{80,48},{96,64},{112,80},{128,96},{144,112}... | collective-permute-start | bytes 196616 | tf_op jit(solution)/shard_map/ppermute | solution.py:12
  151.8 0.8 copy-start.4
  153.8 11.7 %copy-start = (f32[512,512]{1,0:T(8,128)S(1)}, f32[512,512]{1,0:T(8,128)}, u32[]{:S(2)}) copy-start(f32[512,512]{1,0:T(8,128)} %all-gather.14.cloned.1.call-done) | copy-start | bytes 3145732
  153.8 35.3 %all-to-all-start.1 = ((f32[16,32,512]{2,1,0:T(8,128)}), f32[16,32,512]{2,1,0:T(8,128)S(1)}, u32[]{:S(2)}, u32[]{:S(2)}) async-start(f32[16,32,512]{2,1,0:T(8,128)} %stack.11), calls=%async_computation.1 | async-start | bytes 2097152 | tf_op jit(solution)/shard_map/all_to_all | solution.py:38
  158.4 82.6 %all-gather.18.cloned.1.call-start = ((), (), s32[]{:S(2)}) async-start(), calls=%async_computation.8 | async-start | bytes 1114112 | tf_op jit(solution)/shard_map/all_gather | solution.py:34
  158.4 7.1 %collective-permute-start.3 = (f32[32,512]{1,0:T(8,128)S(1)}, f32[32,512]{1,0:T(8,128)S(1)}, u32[]{:S(2)}, u32[]{:S(2)}) collective-permute-start(f32[32,512]{1,0:T(8,128)S(1)} %copy-done.4), channel_id=1, source_target_pairs={{32,0},{48,16},{64,32},{80,48},{96,64},{112,80},{128,96},{144,112}... | collective-permute-start | bytes 196616 | tf_op jit(solution)/shard_map/ppermute | solution.py:12
  166.8 123.5 %all-gather.20.cloned.1.call-start = ((), (), s32[]{:S(2)}) async-start(), calls=%async_computation.9 | async-start | bytes 1114112 | tf_op jit(solution)/shard_map/all_gather | solution.py:44
  200.6 40.5 %collective-permute-start.4 = (f32[32,512]{1,0:T(8,128)S(1)}, f32[32,512]{1,0:T(8,128)S(1)}, u32[]{:S(2)}, u32[]{:S(2)}) collective-permute-start(f32[32,512]{1,0:T(8,128)S(1)} %convolution_add_fusion.3), channel_id=1, source_target_pairs={{64,0},{80,16},{96,32},{112,48},{128,64},{144,80},{160,96},{176,11... | collective-permute-start | bytes 196616 | tf_op jit(solution)/shard_map/ppermute | solution.py:12
  243.6 0.8 copy-start.5
  245.5 10.2 %copy-start.1 = (f32[512,512]{1,0:T(8,128)S(1)}, f32[512,512]{1,0:T(8,128)}, u32[]{:S(2)}) copy-start(f32[512,512]{1,0:T(8,128)} %all-gather.18.cloned.1.call-done) | copy-start | bytes 3145732
  245.5 35.3 %all-to-all-start.2 = ((f32[16,32,512]{2,1,0:T(8,128)}), f32[16,32,512]{2,1,0:T(8,128)S(1)}, u32[]{:S(2)}, u32[]{:S(2)}) async-start(f32[16,32,512]{2,1,0:T(8,128)} %stack.12), calls=%async_computation.2 | async-start | bytes 2097152 | tf_op jit(solution)/shard_map/all_to_all | solution.py:38
  250.1 82.8 %all-gather.22.cloned.1.call-start = ((), (), s32[]{:S(2)}) async-start(), calls=%async_computation.10 | async-start | bytes 1114112 | tf_op jit(solution)/shard_map/all_gather | solution.py:34
  250.2 5.6 %collective-permute-start.5 = (f32[32,512]{1,0:T(8,128)S(1)}, f32[32,512]{1,0:T(8,128)S(1)}, u32[]{:S(2)}, u32[]{:S(2)}) collective-permute-start(f32[32,512]{1,0:T(8,128)S(1)} %copy-done.5), channel_id=1, source_target_pairs={{64,0},{80,16},{96,32},{112,48},{128,64},{144,80},{160,96},{176,11... | collective-permute-start | bytes 196616 | tf_op jit(solution)/shard_map/ppermute | solution.py:12
  257.1 125.1 %all-gather.24.cloned.1.call-start = ((), (), s32[]{:S(2)}) async-start(), calls=%async_computation.11 | async-start | bytes 1114112 | tf_op jit(solution)/shard_map/all_gather | solution.py:44
  292.3 40.6 %collective-permute-start.6 = (f32[32,512]{1,0:T(8,128)S(1)}, f32[32,512]{1,0:T(8,128)S(1)}, u32[]{:S(2)}, u32[]{:S(2)}) collective-permute-start(f32[32,512]{1,0:T(8,128)S(1)} %convolution_add_fusion.2), channel_id=1, source_target_pairs={{128,0},{144,16},{160,32},{176,48},{192,64},{208,80},{224,96},{240... | collective-permute-start | bytes 196616 | tf_op jit(solution)/shard_map/ppermute | solution.py:12
  335.5 0.8 copy-start.6
  337.4 11.1 %copy-start.2 = (f32[512,512]{1,0:T(8,128)S(1)}, f32[512,512]{1,0:T(8,128)}, u32[]{:S(2)}) copy-start(f32[512,512]{1,0:T(8,128)} %all-gather.22.cloned.1.call-done) | copy-start | bytes 3145732
  337.4 35.3 %all-to-all-start.3 = ((f32[16,32,512]{2,1,0:T(8,128)}), f32[16,32,512]{2,1,0:T(8,128)S(1)}, u32[]{:S(2)}, u32[]{:S(2)}) async-start(f32[16,32,512]{2,1,0:T(8,128)} %stack.13), calls=%async_computation.3 | async-start | bytes 2097152 | tf_op jit(solution)/shard_map/all_to_all | solution.py:38
  342.0 87.9 %all-gather.26.cloned.1.call-start = ((), (), s32[]{:S(2)}) async-start(), calls=%async_computation.12 | async-start | bytes 1114112 | tf_op jit(solution)/shard_map/all_gather | solution.py:34
  342.1 6.5 %collective-permute-start.7 = (f32[32,512]{1,0:T(8,128)S(1)}, f32[32,512]{1,0:T(8,128)S(1)}, u32[]{:S(2)}, u32[]{:S(2)}) collective-permute-start(f32[32,512]{1,0:T(8,128)S(1)} %copy-done.6), channel_id=1, source_target_pairs={{128,0},{144,16},{160,32},{176,48},{192,64},{208,80},{224,96},{240... | collective-permute-start | bytes 196616 | tf_op jit(solution)/shard_map/ppermute | solution.py:12
  382.2 3.3 copy-start.7
  384.2 45.6 %collective-permute-start.8 = (f32[32,512]{1,0:T(8,128)S(1)}, f32[32,512]{1,0:T(8,128)S(1)}, u32[]{:S(2)}, u32[]{:S(2)}) collective-permute-start(f32[32,512]{1,0:T(8,128)S(1)} %convolution_add_fusion.1), channel_id=1, source_target_pairs={{256,0},{272,16},{288,32},{304,48},{320,64},{336,80},{352,96},{368... | collective-permute-start | bytes 196616 | tf_op jit(solution)/shard_map/ppermute | solution.py:12
  386.7 45.8 %all-to-all-start.4 = ((f32[16,32,512]{2,1,0:T(8,128)}), f32[16,32,512]{2,1,0:T(8,128)S(1)}, u32[]{:S(2)}, u32[]{:S(2)}) async-start(f32[16,32,512]{2,1,0:T(8,128)} %stack.14), calls=%async_computation.4 | async-start | bytes 2097152 | tf_op jit(solution)/shard_map/all_to_all | solution.py:38
  391.3 84.9 %all-gather.28.cloned.1.call-start = ((), (), s32[]{:S(2)}) async-start(), calls=%async_computation.13 | async-start | bytes 1114112 | tf_op jit(solution)/shard_map/all_gather | solution.py:44
Sparse Core Ops, SparseCore 0:
  9.5 47.8 all-gather.29
  60.1 46.5 all-gather.11
  108.8 40.3 all-gather.13
  152.0 46.5 all-gather.15
  200.6 40.4 all-gather.17
  243.7 46.5 all-gather.19
  292.5 40.4 all-gather.21
  335.6 46.5 all-gather.23
  384.4 45.4 all-gather.25
  432.6 43.5 all-gather.27
